TPU v7x, 512 devices: a whole 4x8x8 slice. The times are simulated.
512 devices in a mesh: dp: 512 (over y, x, z, core).
Axes of the slice: x: 4, y: 8, z: 8, core: 2. Of those that a mesh axis runs over, the one named last changes fastest.
Arguments:
- images: bfloat16 [262144, 1024], P('dp'), may hold values from -0.1875 to 0.1875
- texts: bfloat16 [262144, 1024], P('dp'), may hold values from -0.1875 to 0.1875
- logit_scale: float32 [1], replicated, may hold values from 4 to 12
- logit_bias: float32 [1], replicated, may hold values from -6 to -2
Outputs:
- grad_images: bfloat16 [262144, 1024], P('dp')
- grad_texts: bfloat16 [262144, 1024], P('dp')
All inputs are finite; a program needn't handle non-finite values.
Results may differ from a plain program's by a relative error of at most 0.0065.
Values may be sent and summed in bfloat16 or wider, within the bound.
A program may use at most 64 MiB of HBM per device.

v0:
```python
import jax
import jax.numpy as jnp
from jax import lax
from jax.sharding import PartitionSpec as P

EPS = 1e-06


def passed_along(x, axis, by):
    devices = lax.axis_size(axis)
    return lax.ppermute(x, axis, [(i, (i + by) % devices) for i in range(devices)])


def unit_rows(rows):
    wide = rows.astype(jnp.float32)
    inverse = lax.rsqrt(jnp.sum(wide * wide, axis=1, keepdims=True) + EPS)
    unit = wide * inverse
    return (unit, unit.astype(jnp.bfloat16), inverse)


def pair_terms(img_cast, txt_cast, scale, offset, own):
    logits = scale * jnp.dot(img_cast, txt_cast.T, preferred_element_type=jnp.float32) + offset
    if own:
        rows_idx = lax.broadcasted_iota(jnp.int32, logits.shape, 0)
        cols_idx = lax.broadcasted_iota(jnp.int32, logits.shape, 1)
        signs = jnp.where(rows_idx == cols_idx, jnp.float32(1.0), jnp.float32(-1.0))
        slope = -signs * jax.nn.sigmoid(-signs * logits)
    else:
        slope = jax.nn.sigmoid(logits)
    weights = (scale * slope).astype(jnp.bfloat16)
    img_part = jnp.dot(weights, txt_cast, preferred_element_type=jnp.float32)
    txt_part = lax.dot_general(
        weights, img_cast, (((0,), (0,)), ((), ())), preferred_element_type=jnp.float32
    )
    return (img_part, txt_part)


def unnormalize(grad, unit, inverse):
    return (inverse * (grad - unit * jnp.sum(unit * grad, axis=1, keepdims=True))).astype(
        jnp.bfloat16
    )


def shards(images, texts, logit_scale, logit_bias):
    scale = logit_scale[0]
    offset = logit_bias[0]
    img_unit, img_cast, img_inv = unit_rows(images)
    txt_unit, txt_cast, txt_inv = unit_rows(texts)
    img_zero, txt_zero = pair_terms(img_cast, txt_cast, scale, offset, True)
    nearer = passed_along(txt_cast, "dp", 1)
    img_first, txt_first = pair_terms(img_cast, nearer, scale, offset, False)
    farther = passed_along(nearer, "dp", 1)
    img_second, txt_second = pair_terms(img_cast, farther, scale, offset, False)
    back_first = txt_first.astype(jnp.bfloat16)
    back_second = txt_second.astype(jnp.bfloat16)
    home_first = passed_along(back_first, "dp", -1)
    home_second = passed_along(back_second, "dp", -2)
    own_part = lax.optimization_barrier(txt_zero.astype(jnp.bfloat16)).astype(jnp.float32)
    text_grad = own_part + home_first.astype(jnp.float32) + home_second.astype(jnp.float32)
    image_grad = img_zero + img_first + img_second
    grad_images = unnormalize(image_grad, img_unit, img_inv)
    grad_texts = unnormalize(text_grad, txt_unit, txt_inv)
    return (grad_images, grad_texts)


def solution(mesh):
    in_specs = (P("dp", None), P("dp", None), P(), P())
    out_specs = (P("dp", None), P("dp", None))
    return jax.shard_map(shards, mesh=mesh, in_specs=in_specs, out_specs=out_specs, check_vma=False)
```

profile of v0, /device:TPU:1, one launch (start us, length us, event | category | flops | bytes accessed | tf_op | source)
XLA Modules:
  0.0 82.7 jit_solution(895569830686748390)
XLA Ops:
  0.6 0.0 copy-start.1
  0.6 1.6 %fusion.15 = f32[512]{0:T(512)S(1)} fusion(bf16[512,1024]{1,0:T(8,128)(2,1)} %param.5), kind=kLoop, calls=%fused_computation.19 | loop fusion | flops 1572352 | bytes 1050624 | tf_op jit(solution)/shard_map/reduce_sum | solution.py:16
  2.2 1.5 %fusion.2 = bf16[512,1024]{1,0:T(8,128)(2,1)S(1)} fusion(bf16[512,1024]{1,0:T(8,128)(2,1)} %param.5, f32[512]{0:T(512)S(1)} %add_rsqrt_fusion), kind=kLoop, calls=%fused_computation.4 | loop fusion | flops 1572864 | bytes 2099200 | tf_op jit(solution)/shard_map/convert_element_type | solution.py:18
  3.7 5.4 %collective-permute-start = (bf16[512,1024]{1,0:T(8,128)(2,1)S(1)}, bf16[512,1024]{1,0:T(8,128)(2,1)S(1)}, u32[]{:S(2)}, u32[]{:S(2)}) collective-permute-start(bf16[512,1024]{1,0:T(8,128)(2,1)S(1)} %fusion.2), channel_id=1, source_target_pairs={{0,1},{1,2},{2,3},{3,4},{4,5},{5,6},{6,7},{7,8},{8,9},{9,10},{10,1... | collective-permute-start | bytes 3145736 | tf_op jit(solution)/shard_map/ppermute | solution.py:11
  10.4 0.0 copy-done.1
  10.4 0.3 fusion.10
  10.7 1.0 %fusion.36 = bf16[512,512]{1,0:T(8,128)(2,1)S(1)} fusion(bf16[512,1024]{1,0:T(8,128)(2,1)S(1)} %fusion.2, f32[]{:T(128)} %bitcast.17, f32[]{:T(128)} %bitcast.16, bf16[512,1024]{1,0:T(8,128)(2,1)S(1)} %copy-done.1, f32[512]{0:T(512)S(1)} %add_rsqrt_fusion.1), kind=kOutput, calls=%fused_computation.48 | convolution fusion | flops 541589504 | bytes 2623496 | tf_op jit(solution)/shard_map/dot_general | solution.py:22
  11.7 9.2 %collective-permute-done = bf16[512,1024]{1,0:T(8,128)(2,1)S(1)} collective-permute-done((bf16[512,1024]{1,0:T(8,128)(2,1)S(1)}, bf16[512,1024]{1,0:T(8,128)(2,1)S(1)}, u32[]{:S(2)}, u32[]{:S(2)}) %collective-permute-start) | collective-permute-done | bytes 1048608 | tf_op jit(solution)/shard_map/ppermute | solution.py:11
  20.8 4.4 %collective-permute-start.1 = (bf16[512,1024]{1,0:T(8,128)(2,1)S(1)}, bf16[512,1024]{1,0:T(8,128)(2,1)S(1)}, u32[]{:S(2)}, u32[]{:S(2)}) collective-permute-start(bf16[512,1024]{1,0:T(8,128)(2,1)S(1)} %collective-permute-done), channel_id=1, source_target_pairs={{0,1},{1,2},{2,3},{3,4},{4,5},{5,6},{6,7},{7,8},{8,9},{9,10},{10,1... | collective-permute-start | bytes 3145736 | tf_op jit(solution)/shard_map/ppermute | solution.py:11
  25.2 0.8 %convolution_convert_fusion.2 = bf16[512,1024]{1,0:T(8,128)(2,1)S(1)} fusion(bf16[512,512]{1,0:T(8,128)(2,1)S(1)} %fusion.36, bf16[512,1024]{1,0:T(8,128)(2,1)S(1)} %copy-done.1, f32[512]{0:T(512)S(1)} %add_rsqrt_fusion.1), kind=kOutput, calls=%fused_computation.24 | convolution fusion | flops 538968064 | bytes 2623488 | tf_op jit(solution)/shard_map/dot_general | solution.py:32
  26.1 0.7 fusion.45
  26.8 0.9 %fusion.38 = bf16[512,512]{1,0:T(8,128)(2,1)S(1)} fusion(bf16[512,1024]{1,0:T(8,128)(2,1)S(1)} %collective-permute-done, f32[]{:T(128)} %bitcast.19, f32[]{:T(128)} %bitcast.14, bf16[512,1024]{1,0:T(8,128)(2,1)S(1)} %copy-done.1, f32[512]{0:T(512)S(1)} %add_rsqrt_fusion.1), kind=kOutput, calls=%fused_computation.50 | convolution fusion | flops 540278784 | bytes 2623496 | tf_op jit(solution)/shard_map/dot_general | solution.py:22
  27.7 0.8 %convolution_convert_fusion.1 = bf16[512,1024]{1,0:T(8,128)(2,1)S(1)} fusion(bf16[512,512]{1,0:T(8,128)(2,1)S(1)} %fusion.38, bf16[512,1024]{1,0:T(8,128)(2,1)S(1)} %copy-done.1, f32[512]{0:T(512)S(1)} %add_rsqrt_fusion.1), kind=kOutput, calls=%fused_computation.23 | convolution fusion | flops 538968064 | bytes 2623488 | tf_op jit(solution)/shard_map/dot_general | solution.py:32
  28.5 11.8 %collective-permute-start.2 = (bf16[512,1024]{1,0:T(8,128)(2,1)S(1)}, bf16[512,1024]{1,0:T(8,128)(2,1)S(1)}, u32[]{:S(2)}, u32[]{:S(2)}) collective-permute-start(bf16[512,1024]{1,0:T(8,128)(2,1)S(1)} %convolution_convert_fusion.1), channel_id=1, source_target_pairs={{0,511},{1,0},{2,1},{3,2},{4,3},{5,4},{6,5},{7,6},{8,7},{9,8},{10,... | collective-permute-start | bytes 3145736 | tf_op jit(solution)/shard_map/ppermute | solution.py:11
  40.3 0.0 collective-permute-done.1
  40.3 0.9 %fusion.37 = bf16[512,512]{1,0:T(8,128)(2,1)S(1)} fusion(bf16[512,1024]{1,0:T(8,128)(2,1)S(1)} %collective-permute-done.1, f32[]{:T(128)} %bitcast.18, f32[]{:T(128)} %bitcast.15, bf16[512,1024]{1,0:T(8,128)(2,1)S(1)} %copy-done.1, f32[512]{0:T(512)S(1)} %add_rsqrt_fusion.1), kind=kOutput, calls=%fused_computation.49 | convolution fusion | flops 540278784 | bytes 2623496 | tf_op jit(solution)/shard_map/dot_general | solution.py:22
  41.3 0.8 %convolution_convert_fusion = bf16[512,1024]{1,0:T(8,128)(2,1)S(1)} fusion(bf16[512,512]{1,0:T(8,128)(2,1)S(1)} %fusion.37, bf16[512,1024]{1,0:T(8,128)(2,1)S(1)} %copy-done.1, f32[512]{0:T(512)S(1)} %add_rsqrt_fusion.1), kind=kOutput, calls=%fused_computation.22 | convolution fusion | flops 538968064 | bytes 2623488 | tf_op jit(solution)/shard_map/dot_general | solution.py:32
  42.1 15.1 %collective-permute-start.3 = (bf16[512,1024]{1,0:T(8,128)(2,1)S(1)}, bf16[512,1024]{1,0:T(8,128)(2,1)S(1)}, u32[]{:S(2)}, u32[]{:S(2)}) collective-permute-start(bf16[512,1024]{1,0:T(8,128)(2,1)S(1)} %convolution_convert_fusion), channel_id=1, source_target_pairs={{0,510},{1,511},{2,0},{3,1},{4,2},{5,3},{6,4},{7,5},{8,6},{9,7},{1... | collective-permute-start | bytes 3145736 | tf_op jit(solution)/shard_map/ppermute | solution.py:11
  57.2 0.7 fusion.46
  58.0 1.0 %fusion.6 = (f32[512]{0:T(512)S(1)}, f32[512,1024]{1,0:T(8,128)S(1)}) fusion(bf16[512,1024]{1,0:T(8,128)(2,1)S(1)} %copy-done.1, f32[512]{0:T(512)S(1)} %add_rsqrt_fusion.1, bf16[512,512]{1,0:T(8,128)(2,1)S(1)} %fusion.37, bf16[512,1024]{1,0:T(8,128)(2,1)S(1)} %collective-permute-done.1, f32[512,1024]{1,0:T(8,128)S(1)} %fusion.45, f32[512,1024]{1,0:T(8,128)S(1)} %fusion.46), kind=kOutput, calls=%fused_computation.10 | convolution fusion | flops 540016128 | bytes 8916992 | tf_op jit(solution)/shard_map/dot_general | solution.py:31
  59.0 0.0 copy-start
  59.0 1.4 %fusion.9 = bf16[512,1024]{1,0:T(8,128)(2,1)} fusion(f32[512,1024]{1,0:T(8,128)S(1)} %get-tuple-element.3, bf16[512,1024]{1,0:T(8,128)(2,1)S(1)} %copy-done.1, f32[512]{0:T(512)S(1)} %get-tuple-element.2, f32[512]{0:T(512)S(1)} %add_rsqrt_fusion.1), kind=kLoop, calls=%fused_computation.13 | loop fusion | flops 3145728 | bytes 4198400 | tf_op jit(solution)/shard_map/convert_element_type | solution.py:39
  60.4 0.0 collective-permute-done.2
  60.4 19.9 %collective-permute-done.3 = bf16[512,1024]{1,0:T(8,128)(2,1)S(1)} collective-permute-done((bf16[512,1024]{1,0:T(8,128)(2,1)S(1)}, bf16[512,1024]{1,0:T(8,128)(2,1)S(1)}, u32[]{:S(2)}, u32[]{:S(2)}) %collective-permute-start.3) | collective-permute-done | bytes 1048608 | tf_op jit(solution)/shard_map/ppermute | solution.py:11
  80.3 0.0 copy-done
  80.3 0.7 fusion.11
  81.0 1.7 %fusion.14 = bf16[512,1024]{1,0:T(8,128)(2,1)} fusion(bf16[512,1024]{1,0:T(8,128)(2,1)S(1)} %copy-done, bf16[512,1024]{1,0:T(8,128)(2,1)S(1)} %collective-permute-done.3, bf16[512,1024]{1,0:T(8,128)(2,1)S(1)} %collective-permute-done.2, bf16[512,1024]{1,0:T(8,128)(2,1)S(1)} %convolution_convert_fusion.2, f32[512]{0:T(512)S(1)} %fusion.11, ...), kind=kLoop, calls=%fused_computation.18 | loop fusion | flops 5767168 | bytes 5246976 | tf_op jit(solution)/shard_map/convert_element_type | solution.py:39
  (2 shorter events, 0.0 us)
Async XLA Ops:
  0.6 9.8 %copy-start.1 = (bf16[512,1024]{1,0:T(8,128)(2,1)S(1)}, bf16[512,1024]{1,0:T(8,128)(2,1)}, u32[]{:S(2)}) copy-start(bf16[512,1024]{1,0:T(8,128)(2,1)} %param.4) | copy-start | bytes 3145732
  3.7 17.1 %collective-permute-start = (bf16[512,1024]{1,0:T(8,128)(2,1)S(1)}, bf16[512,1024]{1,0:T(8,128)(2,1)S(1)}, u32[]{:S(2)}, u32[]{:S(2)}) collective-permute-start(bf16[512,1024]{1,0:T(8,128)(2,1)S(1)} %fusion.2), channel_id=1, source_target_pairs={{0,1},{1,2},{2,3},{3,4},{4,5},{5,6},{6,7},{7,8},{8,9},{9,10},{10,1... | collective-permute-start | bytes 3145736 | tf_op jit(solution)/shard_map/ppermute | solution.py:11
  20.8 19.5 %collective-permute-start.1 = (bf16[512,1024]{1,0:T(8,128)(2,1)S(1)}, bf16[512,1024]{1,0:T(8,128)(2,1)S(1)}, u32[]{:S(2)}, u32[]{:S(2)}) collective-permute-start(bf16[512,1024]{1,0:T(8,128)(2,1)S(1)} %collective-permute-done), channel_id=1, source_target_pairs={{0,1},{1,2},{2,3},{3,4},{4,5},{5,6},{6,7},{7,8},{8,9},{9,10},{10,1... | collective-permute-start | bytes 3145736 | tf_op jit(solution)/shard_map/ppermute | solution.py:11
  28.5 31.8 %collective-permute-start.2 = (bf16[512,1024]{1,0:T(8,128)(2,1)S(1)}, bf16[512,1024]{1,0:T(8,128)(2,1)S(1)}, u32[]{:S(2)}, u32[]{:S(2)}) collective-permute-start(bf16[512,1024]{1,0:T(8,128)(2,1)S(1)} %convolution_convert_fusion.1), channel_id=1, source_target_pairs={{0,511},{1,0},{2,1},{3,2},{4,3},{5,4},{6,5},{7,6},{8,7},{9,8},{10,... | collective-permute-start | bytes 3145736 | tf_op jit(solution)/shard_map/ppermute | solution.py:11
  42.1 38.2 %collective-permute-start.3 = (bf16[512,1024]{1,0:T(8,128)(2,1)S(1)}, bf16[512,1024]{1,0:T(8,128)(2,1)S(1)}, u32[]{:S(2)}, u32[]{:S(2)}) collective-permute-start(bf16[512,1024]{1,0:T(8,128)(2,1)S(1)} %convolution_convert_fusion), channel_id=1, source_target_pairs={{0,510},{1,511},{2,0},{3,1},{4,2},{5,3},{6,4},{7,5},{8,6},{9,7},{1... | collective-permute-start | bytes 3145736 | tf_op jit(solution)/shard_map/ppermute | solution.py:11
  59.0 21.3 %copy-start = (bf16[512,1024]{1,0:T(8,128)(2,1)S(1)}, bf16[512,1024]{1,0:T(8,128)(2,1)}, u32[]{:S(2)}) copy-start(bf16[512,1024]{1,0:T(8,128)(2,1)} %param.5) | copy-start | bytes 3145732
where the time goes:
time: 83 us; the launch traced here: 82.7 us
  starting transfers between devices  36.7 us (44%)
  waiting for transfers between devices  29.1 us (35%)
  matrix products  7.69 us (9%)
  other arithmetic  7.21 us (9%)
  between operations  2.05 us (2%)
    ppermute x4, starting transfers between devices, passed_along(): lax.ppermute(x, axis, [(i, (i + by) % devices) for i in range(devices)])  36.7 us
    ppermute x4, waiting for transfers between devices, passed_along(): lax.ppermute(x, axis, [(i, (i + by) % devices) for i in range(devices)])  29.1 us
    convert_element_type x2, other arithmetic, unnormalize(): (inverse * (grad - unit * jnp.sum(unit * grad, axis=1, keepdims=True))).a...  3.12 us
    dot_general x3, matrix products, pair_terms(): jnp.dot(img_cast, txt_cast.T, preferred_element_type=jnp.float32)  2.76 us
    dot_general x3, matrix products, pair_terms(): lax.dot_general(weights, img_cast, (((0,), (0,)), ((), ())), preferred_el...  2.5 us
    dot_general x3, matrix products, pair_terms(): img_part = jnp.dot(weights, txt_cast, preferred_element_type=jnp.float32)  2.44 us
    reduce_sum x2, other arithmetic, unit_rows(): inverse = lax.rsqrt(jnp.sum(wide * wide, axis=1, keepdims=True) + EPS)  1.87 us
  transfers between devices with their start and end apart: 4, of which 2 were waited for; matrix products, arithmetic and copies ran while one was open for 11% of the time, Pallas kernels for 0%

commit v1 on v0

v1 whole, which is shorter than its diff:
```python
import functools

import jax
import jax.numpy as jnp
from jax import lax
from jax.experimental import pallas as pl
from jax.experimental.pallas import tpu as pltpu
from jax.sharding import PartitionSpec as P

EPS = 1e-06
MESH = pl.DeviceIdType.MESH
TILE = 256
NEAR_ROWS = 128
FAR_ROWS = 64


def kernel(
    n,
    img_ref,
    txt_ref,
    scale_ref,
    bias_ref,
    gi_ref,
    gt_ref,
    u_raw,
    v_raw,
    chip_raw,
    near_raw,
    relay_raw,
    far_raw,
    u_unit,
    v_unit,
    block_unit,
    u_inv,
    v_inv,
    u_grad,
    v_grad,
    u_out,
    v_out,
    load_sem,
    chip_send,
    chip_recv,
    near_send,
    near_recv,
    relay_send,
    relay_recv,
    far_send,
    far_recv,
    store_sem,
):
    rows, depth = u_raw.shape
    me = lax.axis_index("dp")
    core = lax.rem(me, 2)
    partner = me + 1 - 2 * core
    near_to = lax.rem(me + 4 * core - 2 + n, n)
    far_to = lax.rem(me + 2 * core - 1 + n, n)
    scale = scale_ref[0]
    bias = bias_ref[0]

    barrier = pltpu.get_barrier_semaphore()
    for by in (-2, -1, 1, 2):
        pl.semaphore_signal(
            barrier, inc=1, device_id=(lax.rem(me + by + n, n),), device_id_type=MESH
        )

    def on_core(which, texts, images):
        @pl.when(core == which)
        def _():
            load_u = pltpu.make_async_copy(texts, u_raw, load_sem.at[0])
            load_v = pltpu.make_async_copy(images, v_raw, load_sem.at[1])
            load_u.start()
            load_v.start()
            pl.semaphore_wait(barrier, 4)
            send_chip(texts).start()
            for k in range(rows // NEAR_ROWS):
                send_near(images, k).start()

    def send_chip(source):
        return pltpu.make_async_remote_copy(
            src_ref=source,
            dst_ref=chip_raw,
            send_sem=chip_send.at[0],
            recv_sem=chip_recv.at[0],
            device_id=(partner,),
            device_id_type=MESH,
        )

    def send_near(source, k):
        part = pl.ds(k * NEAR_ROWS, NEAR_ROWS)
        return pltpu.make_async_remote_copy(
            src_ref=source.at[part],
            dst_ref=near_raw.at[part],
            send_sem=near_send.at[k],
            recv_sem=near_recv.at[k],
            device_id=(near_to,),
            device_id_type=MESH,
        )

    def send_relay(k):
        part = pl.ds(k * NEAR_ROWS, NEAR_ROWS)
        return pltpu.make_async_remote_copy(
            src_ref=near_raw.at[part],
            dst_ref=relay_raw.at[part],
            send_sem=relay_send.at[k],
            recv_sem=relay_recv.at[k],
            device_id=(partner,),
            device_id_type=MESH,
        )

    def send_far(k):
        part = pl.ds(k * FAR_ROWS, FAR_ROWS)
        return pltpu.make_async_remote_copy(
            src_ref=chip_raw.at[part],
            dst_ref=far_raw.at[part],
            send_sem=far_send.at[k],
            recv_sem=far_recv.at[k],
            device_id=(far_to,),
            device_id_type=MESH,
        )

    on_core(0, txt_ref, img_ref)
    on_core(1, img_ref, txt_ref)

    def normalize(raw, unit, start, count, inverses=None):
        for at in range(start, start + count, 64):
            part = pl.ds(at, min(64, count))
            wide = raw[part, :].astype(jnp.float32)
            inverse = lax.rsqrt(jnp.sum(wide * wide, axis=1, keepdims=True) + EPS)
            unit[part, :] = (wide * inverse).astype(jnp.bfloat16)
            if inverses is not None:
                inverses[part, :] = jnp.broadcast_to(inverse, (part.size, inverses.shape[1]))

    def accumulate(own, block, start, count, grad, diagonal=False, first=False):
        part = block[pl.ds(start, count), :]
        for at in range(0, rows, TILE):
            here = pl.ds(at, TILE)
            logits = scale * lax.dot_general(
                own[here, :], part, (((1,), (1,)), ((), ())), preferred_element_type=jnp.float32
            ) + bias
            if diagonal and at == start:
                down = lax.broadcasted_iota(jnp.int32, logits.shape, 0)
                across = lax.broadcasted_iota(jnp.int32, logits.shape, 1)
                signs = jnp.where(down == across, jnp.float32(1.0), jnp.float32(-1.0))
                slope = -signs * jax.nn.sigmoid(-signs * logits)
            else:
                slope = jax.nn.sigmoid(logits)
            weights = (scale * slope).astype(jnp.bfloat16)
            term = jnp.dot(weights, part, preferred_element_type=jnp.float32)
            grad[here, :] = term if first else grad[here, :] + term

    def finish(grad, raw, inverses, out):
        for at in range(0, rows, 64):
            here = pl.ds(at, 64)
            inverse = inverses[here, 0:1]
            wide = grad[here, :]
            unit = raw[here, :].astype(jnp.float32) * inverse
            along = jnp.sum(unit * wide, axis=1, keepdims=True)
            out[here, :] = (inverse * (wide - unit * along)).astype(jnp.bfloat16)

    pltpu.make_async_copy(txt_ref, u_raw, load_sem.at[0]).wait()
    pltpu.make_async_copy(img_ref, v_raw, load_sem.at[1]).wait()
    normalize(u_raw, u_unit, 0, rows, u_inv)
    normalize(v_raw, v_unit, 0, rows, v_inv)
    for start in range(0, rows, TILE):
        accumulate(u_unit, v_unit, start, TILE, u_grad, diagonal=True, first=start == 0)
        accumulate(v_unit, u_unit, start, TILE, v_grad, diagonal=True, first=start == 0)

    send_chip(txt_ref).wait_recv()
    normalize(chip_raw, block_unit, 0, rows)
    for start in range(0, rows, TILE):
        accumulate(u_unit, block_unit, start, TILE, u_grad)

    per_tile = TILE // NEAR_ROWS
    nears = rows // NEAR_ROWS
    fars = rows // FAR_ROWS
    for tile in range(rows // TILE):
        for k in range(tile * per_tile, (tile + 1) * per_tile):
            send_near(img_ref, k).wait_recv()
            send_relay(k).start()
            normalize(near_raw, block_unit, k * NEAR_ROWS, NEAR_ROWS)
        accumulate(u_unit, block_unit, tile * TILE, TILE, u_grad)
    for k in range(nears):
        send_near(img_ref, k).wait_send()
        if k == nears - 2:
            for j in range(2):
                send_far(j).start()
    for tile in range(rows // TILE):
        for k in range(tile * per_tile, (tile + 1) * per_tile):
            send_relay(k).wait_recv()
            normalize(relay_raw, block_unit, k * NEAR_ROWS, NEAR_ROWS)
        accumulate(v_unit, block_unit, tile * TILE, TILE, v_grad)
    finish(u_grad, u_raw, u_inv, u_out)

    def store(source, out, slot):
        return pltpu.make_async_copy(source, out, store_sem.at[slot])

    @pl.when(core == 0)
    def _():
        store(u_out, gt_ref, 0).start()

    @pl.when(core == 1)
    def _():
        store(u_out, gi_ref, 0).start()

    for k in range(fars):
        send_far(k).wait_send()
        if k + 2 < fars:
            send_far(k + 2).start()
        send_far(k).wait_recv()
        normalize(far_raw, block_unit, k * FAR_ROWS, FAR_ROWS)
        accumulate(v_unit, block_unit, k * FAR_ROWS, FAR_ROWS, v_grad)
    finish(v_grad, v_raw, v_inv, v_out)

    @pl.when(core == 0)
    def _():
        store(v_out, gi_ref, 1).start()

    @pl.when(core == 1)
    def _():
        store(v_out, gt_ref, 1).start()

    for k in range(nears):
        send_relay(k).wait_send()
    send_chip(txt_ref).wait_send()
    store(u_out, gt_ref, 0).wait()
    store(v_out, gi_ref, 1).wait()


def solution(mesh):
    n = mesh.shape["dp"]

    def shards(images, texts, logit_scale, logit_bias):
        rows, depth = images.shape
        block = pltpu.VMEM((rows, depth), jnp.bfloat16)
        total = pltpu.VMEM((rows, depth), jnp.float32)
        inverses = pltpu.VMEM((rows, 128), jnp.float32)
        dma = pltpu.SemaphoreType.DMA
        nears, fars = rows // NEAR_ROWS, rows // FAR_ROWS
        result = jax.ShapeDtypeStruct((rows, depth), jnp.bfloat16)
        return pl.pallas_call(
            functools.partial(kernel, n),
            out_shape=(result, result),
            in_specs=[pl.BlockSpec(memory_space=pl.ANY)] * 2
            + [pl.BlockSpec(memory_space=pltpu.SMEM)] * 2,
            out_specs=[pl.BlockSpec(memory_space=pl.ANY)] * 2,
            scratch_shapes=[block] * 6
            + [block] * 3
            + [inverses] * 2
            + [total] * 2
            + [block] * 2
            + [
                dma((2,)),
                dma((1,)),
                dma((1,)),
                dma((nears,)),
                dma((nears,)),
                dma((nears,)),
                dma((nears,)),
                dma((fars,)),
                dma((fars,)),
                dma((2,)),
            ],
            compiler_params=pltpu.CompilerParams(
                collective_id=0, has_side_effects=True, vmem_limit_bytes=48 * 1024 * 1024
            ),
            cost_estimate=pl.CostEstimate(
                flops=24 * rows * rows * depth, bytes_accessed=8 * rows * depth, transcendentals=0
            ),
        )(images, texts, logit_scale, logit_bias)

    in_specs = (P("dp", None), P("dp", None), P(), P())
    out_specs = (P("dp", None), P("dp", None))
    return jax.shard_map(shards, mesh=mesh, in_specs=in_specs, out_specs=out_specs, check_vma=False)
```

time: 83 us -> 53.8 us (0.65)
  the two profiles are of different devices: /device:TPU:1 before, /device:TPU:32 now
where the time goes in v1:
time: 53.8 us; the launch traced here: 53.6 us
  Pallas kernels  47.3 us (88%)
  local copies, waits for them, and re-layouts  4.38 us (8%)
  between operations  1.94 us (4%)
    pallas_call x1, Pallas kernels, shards(): pl.pallas_call(functools.partial(kernel, n), out_shape=(result, result),...  47.3 us
    unnamed x6, local copies, waits for them, and re-layouts  4.38 us

profile of v1, /device:TPU:32, one launch (start us, length us, event | category | flops | bytes accessed | tf_op | source)
XLA Modules:
  0.0 53.6 jit_solution(17220936277343891795)
XLA Ops:
  1.9 0.0 copy-start
  1.9 1.2 %copy-done = bf16[512,1024]{1,0:T(8,128)(2,1)S(1)} copy-done((bf16[512,1024]{1,0:T(8,128)(2,1)S(1)}, bf16[512,1024]{1,0:T(8,128)(2,1)}, u32[]{:S(2)}) %copy-start) | copy-done | bytes 1048600
  3.1 0.0 copy-start.1
  3.1 1.2 %copy-done.1 = bf16[512,1024]{1,0:T(8,128)(2,1)S(1)} copy-done((bf16[512,1024]{1,0:T(8,128)(2,1)S(1)}, bf16[512,1024]{1,0:T(8,128)(2,1)}, u32[]{:S(2)}) %copy-start.1) | copy-done | bytes 1048600
  4.4 47.3 %shard_map.59 = (bf16[512,1024]{1,0:T(8,128)(2,1)S(1)}, bf16[512,1024]{1,0:T(8,128)(2,1)S(1)}) custom-call(bf16[512,1024]{1,0:T(8,128)(2,1)S(1)} %copy-done, bf16[512,1024]{1,0:T(8,128)(2,1)S(1)} %copy-done.1, f32[1]{0:T(128)S(6)} %copy.8.scale_ref, f32[1]{0:T(128)S(6)} %copy.9.bias_ref), custom_call_target="tpu_custom_call" | custom-call | flops 6442450944 | bytes 4194304 | tf_op jit(solution)/shard_map/pallas_call | solution.py:240
  51.6 1.0 %copy.10 = bf16[512,1024]{1,0:T(8,128)(2,1)} copy(bf16[512,1024]{1,0:T(8,128)(2,1)S(1)} %get-tuple-element.4) | data formatting | bytes 2097152
  52.6 1.0 %copy.11 = bf16[512,1024]{1,0:T(8,128)(2,1)} copy(bf16[512,1024]{1,0:T(8,128)(2,1)S(1)} %get-tuple-element.5) | data formatting | bytes 2097152
Async XLA Ops:
  1.9 1.2 %copy-start = (bf16[512,1024]{1,0:T(8,128)(2,1)S(1)}, bf16[512,1024]{1,0:T(8,128)(2,1)}, u32[]{:S(2)}) copy-start(bf16[512,1024]{1,0:T(8,128)(2,1)} %img_ref.1) | copy-start | bytes 3145732
  3.1 1.2 %copy-start.1 = (bf16[512,1024]{1,0:T(8,128)(2,1)S(1)}, bf16[512,1024]{1,0:T(8,128)(2,1)}, u32[]{:S(2)}) copy-start(bf16[512,1024]{1,0:T(8,128)(2,1)} %txt_ref.1) | copy-start | bytes 3145732

commit v2 on v1

--- a/solution.py
+++ b/solution.py
@@ -12,6 +12,42 @@
 TILE = 256
 NEAR_ROWS = 128
 FAR_ROWS = 64
+STORE_ROWS = 128
+
+
+def finish(grad, raw, inverses, out, start, count):
+    for at in range(start, start + count, 64):
+        here = pl.ds(at, 64)
+        inverse = inverses[here, 0:1]
+        wide = grad[here, :]
+        unit = raw[here, :].astype(jnp.float32) * inverse
+        along = jnp.sum(unit * wide, axis=1, keepdims=True)
+        out[here, :] = (inverse * (wide - unit * along)).astype(jnp.bfloat16)
+
+
+def finish_kernel(u_out, v_grad, v_raw, v_inv, gi_ref, gt_ref, v_out, u_sem, v_sem):
+    core = lax.rem(lax.axis_index("dp"), 2)
+    rows = v_grad.shape[0]
+
+    def store(u_target, v_target):
+        pltpu.make_async_copy(u_out, u_target, u_sem).start()
+        for slot in range(rows // STORE_ROWS):
+            part = pl.ds(slot * STORE_ROWS, STORE_ROWS)
+            finish(v_grad, v_raw, v_inv, v_out, slot * STORE_ROWS, STORE_ROWS)
+            pltpu.make_async_copy(v_out.at[part], v_target.at[part], v_sem.at[slot]).start()
+
+    @pl.when(core == 0)
+    def _():
+        store(gt_ref, gi_ref)
+
+    @pl.when(core == 1)
+    def _():
+        store(gi_ref, gt_ref)
+
+    pltpu.make_async_copy(u_out, gt_ref, u_sem).wait()
+    for slot in range(rows // STORE_ROWS):
+        part = pl.ds(slot * STORE_ROWS, STORE_ROWS)
+        pltpu.make_async_copy(v_out.at[part], gi_ref.at[part], v_sem.at[slot]).wait()
 
 
 def kernel(
@@ -20,10 +56,11 @@
     txt_ref,
     scale_ref,
     bias_ref,
-    gi_ref,
-    gt_ref,
+    u_out,
+    v_grad,
+    v_raw,
+    v_inv,
     u_raw,
-    v_raw,
     chip_raw,
     near_raw,
     relay_raw,
@@ -32,11 +69,7 @@
     v_unit,
     block_unit,
     u_inv,
-    v_inv,
     u_grad,
-    v_grad,
-    u_out,
-    v_out,
     load_sem,
     chip_send,
     chip_recv,
@@ -46,7 +79,6 @@
     relay_recv,
     far_send,
     far_recv,
-    store_sem,
 ):
     rows, depth = u_raw.shape
     me = lax.axis_index("dp")
@@ -58,10 +90,9 @@
     bias = bias_ref[0]
 
     barrier = pltpu.get_barrier_semaphore()
-    for by in (-2, -1, 1, 2):
-        pl.semaphore_signal(
-            barrier, inc=1, device_id=(lax.rem(me + by + n, n),), device_id_type=MESH
-        )
+    near_from = lax.rem(me + 2 - 4 * core + n, n)
+    for sender in (partner, near_from, far_to):
+        pl.semaphore_signal(barrier, inc=1, device_id=(sender,), device_id_type=MESH)
 
     def on_core(which, texts, images):
         @pl.when(core == which)
@@ -70,7 +101,7 @@
             load_v = pltpu.make_async_copy(images, v_raw, load_sem.at[1])
             load_u.start()
             load_v.start()
-            pl.semaphore_wait(barrier, 4)
+            pl.semaphore_wait(barrier, 3)
             send_chip(texts).start()
             for k in range(rows // NEAR_ROWS):
                 send_near(images, k).start()
@@ -120,6 +151,9 @@
 
     on_core(0, txt_ref, img_ref)
     on_core(1, img_ref, txt_ref)
+    send_chip(txt_ref).wait_recv()
+    for k in range(rows // FAR_ROWS):
+        send_far(k).start()
 
     def normalize(raw, unit, start, count, inverses=None):
         for at in range(start, start + count, 64):
@@ -148,15 +182,6 @@
             term = jnp.dot(weights, part, preferred_element_type=jnp.float32)
             grad[here, :] = term if first else grad[here, :] + term
 
-    def finish(grad, raw, inverses, out):
-        for at in range(0, rows, 64):
-            here = pl.ds(at, 64)
-            inverse = inverses[here, 0:1]
-            wide = grad[here, :]
-            unit = raw[here, :].astype(jnp.float32) * inverse
-            along = jnp.sum(unit * wide, axis=1, keepdims=True)
-            out[here, :] = (inverse * (wide - unit * along)).astype(jnp.bfloat16)
-
     pltpu.make_async_copy(txt_ref, u_raw, load_sem.at[0]).wait()
     pltpu.make_async_copy(img_ref, v_raw, load_sem.at[1]).wait()
     normalize(u_raw, u_unit, 0, rows, u_inv)
@@ -165,7 +190,6 @@
         accumulate(u_unit, v_unit, start, TILE, u_grad, diagonal=True, first=start == 0)
         accumulate(v_unit, u_unit, start, TILE, v_grad, diagonal=True, first=start == 0)
 
-    send_chip(txt_ref).wait_recv()
     normalize(chip_raw, block_unit, 0, rows)
     for start in range(0, rows, TILE):
         accumulate(u_unit, block_unit, start, TILE, u_grad)
@@ -179,51 +203,24 @@
             send_relay(k).start()
             normalize(near_raw, block_unit, k * NEAR_ROWS, NEAR_ROWS)
         accumulate(u_unit, block_unit, tile * TILE, TILE, u_grad)
-    for k in range(nears):
-        send_near(img_ref, k).wait_send()
-        if k == nears - 2:
-            for j in range(2):
-                send_far(j).start()
     for tile in range(rows // TILE):
         for k in range(tile * per_tile, (tile + 1) * per_tile):
             send_relay(k).wait_recv()
             normalize(relay_raw, block_unit, k * NEAR_ROWS, NEAR_ROWS)
         accumulate(v_unit, block_unit, tile * TILE, TILE, v_grad)
-    finish(u_grad, u_raw, u_inv, u_out)
-
-    def store(source, out, slot):
-        return pltpu.make_async_copy(source, out, store_sem.at[slot])
-
-    @pl.when(core == 0)
-    def _():
-        store(u_out, gt_ref, 0).start()
-
-    @pl.when(core == 1)
-    def _():
-        store(u_out, gi_ref, 0).start()
+    finish(u_grad, u_raw, u_inv, u_out, 0, rows)
 
     for k in range(fars):
-        send_far(k).wait_send()
-        if k + 2 < fars:
-            send_far(k + 2).start()
         send_far(k).wait_recv()
         normalize(far_raw, block_unit, k * FAR_ROWS, FAR_ROWS)
         accumulate(v_unit, block_unit, k * FAR_ROWS, FAR_ROWS, v_grad)
-    finish(v_grad, v_raw, v_inv, v_out)
-
-    @pl.when(core == 0)
-    def _():
-        store(v_out, gi_ref, 1).start()
-
-    @pl.when(core == 1)
-    def _():
-        store(v_out, gt_ref, 1).start()
 
     for k in range(nears):
+        send_near(img_ref, k).wait_send()
         send_relay(k).wait_send()
+    for k in range(fars):
+        send_far(k).wait_send()
     send_chip(txt_ref).wait_send()
-    store(u_out, gt_ref, 0).wait()
-    store(v_out, gi_ref, 1).wait()
 
 
 def solution(mesh):
@@ -236,18 +233,19 @@
         inverses = pltpu.VMEM((rows, 128), jnp.float32)
         dma = pltpu.SemaphoreType.DMA
         nears, fars = rows // NEAR_ROWS, rows // FAR_ROWS
-        result = jax.ShapeDtypeStruct((rows, depth), jnp.bfloat16)
-        return pl.pallas_call(
+        in_vmem = pl.BlockSpec(memory_space=pltpu.VMEM)
+        in_hbm = pl.BlockSpec(memory_space=pltpu.HBM)
+        images = pltpu.with_memory_space_constraint(images, pltpu.HBM)
+        texts = pltpu.with_memory_space_constraint(texts, pltpu.HBM)
+        parts = pl.pallas_call(
             functools.partial(kernel, n),
-            out_shape=(result, result),
-            in_specs=[pl.BlockSpec(memory_space=pl.ANY)] * 2
-            + [pl.BlockSpec(memory_space=pltpu.SMEM)] * 2,
-            out_specs=[pl.BlockSpec(memory_space=pl.ANY)] * 2,
-            scratch_shapes=[block] * 6
+            out_shape=(block, total, block, inverses),
+            in_specs=[in_hbm] * 2 + [pl.BlockSpec(memory_space=pltpu.SMEM)] * 2,
+            out_specs=[in_vmem] * 4,
+            scratch_shapes=[block] * 5
             + [block] * 3
-            + [inverses] * 2
-            + [total] * 2
-            + [block] * 2
+            + [inverses]
+            + [total]
             + [
                 dma((2,)),
                 dma((1,)),
@@ -258,15 +256,27 @@
                 dma((nears,)),
                 dma((fars,)),
                 dma((fars,)),
-                dma((2,)),
             ],
             compiler_params=pltpu.CompilerParams(
-                collective_id=0, has_side_effects=True, vmem_limit_bytes=48 * 1024 * 1024
+                collective_id=0, has_side_effects=True, vmem_limit_bytes=40 * 1024 * 1024
             ),
             cost_estimate=pl.CostEstimate(
                 flops=24 * rows * rows * depth, bytes_accessed=8 * rows * depth, transcendentals=0
             ),
         )(images, texts, logit_scale, logit_bias)
+        parts = [pltpu.with_memory_space_constraint(part, pltpu.VMEM) for part in parts]
+        result = jax.ShapeDtypeStruct((rows, depth), jnp.bfloat16)
+        return pl.pallas_call(
+            finish_kernel,
+            out_shape=(result, result),
+            in_specs=[in_vmem] * 4,
+            out_specs=[in_hbm] * 2,
+            scratch_shapes=[block, dma, dma((rows // STORE_ROWS,))],
+            compiler_params=pltpu.CompilerParams(vmem_limit_bytes=16 * 1024 * 1024),
+            cost_estimate=pl.CostEstimate(
+                flops=8 * rows * depth, bytes_accessed=4 * rows * depth, transcendentals=0
+            ),
+        )(*parts)
 
     in_specs = (P("dp", None), P("dp", None), P(), P())
     out_specs = (P("dp", None), P("dp", None))

time: 53.8 us -> 45.4 us (0.84)
  the two profiles are of different devices: /device:TPU:32 before, /device:TPU:1 now
where the time goes in v2:
time: 45.4 us; the launch traced here: 45.3 us
  Pallas kernels  43.2 us (95%)
  between operations  2.09 us (5%)
    pallas_call x1, Pallas kernels, shards(): pl.pallas_call(functools.partial(kernel, n), out_shape=(block, total, blo...  41.2 us
    pallas_call x1, Pallas kernels, shards(): pl.pallas_call(finish_kernel, out_shape=(result, result), in_specs=[in_vm...  1.92 us

profile of v2, /device:TPU:1, one launch (start us, length us, event | category | flops | bytes accessed | tf_op | source)
XLA Modules:
  0.0 45.3 jit_solution(2099372323372140102)
XLA Ops:
  1.9 41.2 %shard_map.59 = (bf16[512,1024]{1,0:T(8,128)(2,1)S(1)}, f32[512,1024]{1,0:T(8,128)S(1)}, bf16[512,1024]{1,0:T(8,128)(2,1)S(1)}, f32[512,128]{1,0:T(8,128)S(1)}) custom-call(bf16[512,1024]{1,0:T(8,128)(2,1)} %img_ref.1, bf16[512,1024]{1,0:T(8,128)(2,1)} %txt_ref.1, f32[1]{0:T(128)S(6)} %copy.6.scale_ref, f32[1]{0:T(128)S(6)} %copy.7.bias_ref), custom_call_target="tpu_custom_call" | custom-call | flops 6442450944 | bytes 4194304 | tf_op jit(solution)/shard_map/pallas_call | solution.py:240
  43.2 1.9 %shard_map.60 = (bf16[512,1024]{1,0:T(8,128)(2,1)}, bf16[512,1024]{1,0:T(8,128)(2,1)}) custom-call(bf16[512,1024]{1,0:T(8,128)(2,1)S(1)} %get-tuple-element.6.u_out, f32[512,1024]{1,0:T(8,128)S(1)} %get-tuple-element.7.v_grad, bf16[512,1024]{1,0:T(8,128)(2,1)S(1)} %get-tuple-element.8.v_raw, f32[512,128]{1,0:T(8,128)S(1)} %get-tuple-element.9.v_inv), custom_call_target="tpu_custom_call" | custom-call | flops 4194304 | bytes 2097152 | tf_op jit(solution)/shard_map/pallas_call | solution.py:269

commit v3 on v2

--- a/solution.py
+++ b/solution.py
@@ -11,41 +11,48 @@
 MESH = pl.DeviceIdType.MESH
 TILE = 256
 NEAR_ROWS = 128
-FAR_ROWS = 64
+FAR_CHUNKS = ((0, 128), (128, 128), (256, 128), (384, 64), (448, 64))
+LAST_ROWS = FAR_CHUNKS[-1][1]
 STORE_ROWS = 128
 
 
-def finish(grad, raw, inverses, out, start, count):
-    for at in range(start, start + count, 64):
-        here = pl.ds(at, 64)
-        inverse = inverses[here, 0:1]
-        wide = grad[here, :]
-        unit = raw[here, :].astype(jnp.float32) * inverse
-        along = jnp.sum(unit * wide, axis=1, keepdims=True)
-        out[here, :] = (inverse * (wide - unit * along)).astype(jnp.bfloat16)
-
-
-def finish_kernel(u_out, v_grad, v_raw, v_inv, gi_ref, gt_ref, v_out, u_sem, v_sem):
+def finish(wide, raw, inverse):
+    unit = raw.astype(jnp.float32) * inverse
+    along = jnp.sum(unit * wide, axis=1, keepdims=True)
+    return (inverse * (wide - unit * along)).astype(jnp.bfloat16)
+
+
+def finish_kernel(
+    u_out, v_grad, v_raw, v_inv, last_unit, last_weights, gi_ref, gt_ref, v_out, u_sem, v_sem
+):
     core = lax.rem(lax.axis_index("dp"), 2)
-    rows = v_grad.shape[0]
-
-    def store(u_target, v_target):
-        pltpu.make_async_copy(u_out, u_target, u_sem).start()
-        for slot in range(rows // STORE_ROWS):
-            part = pl.ds(slot * STORE_ROWS, STORE_ROWS)
-            finish(v_grad, v_raw, v_inv, v_out, slot * STORE_ROWS, STORE_ROWS)
-            pltpu.make_async_copy(v_out.at[part], v_target.at[part], v_sem.at[slot]).start()
+    slots = v_grad.shape[0] // STORE_ROWS
 
     @pl.when(core == 0)
     def _():
-        store(gt_ref, gi_ref)
+        pltpu.make_async_copy(u_out, gt_ref, u_sem).start()
 
     @pl.when(core == 1)
     def _():
-        store(gi_ref, gt_ref)
+        pltpu.make_async_copy(u_out, gi_ref, u_sem).start()
+
+    for slot in range(slots):
+        part = pl.ds(slot * STORE_ROWS, STORE_ROWS)
+        wide = v_grad[part, :] + jnp.dot(
+            last_weights[part, :], last_unit[...], preferred_element_type=jnp.float32
+        )
+        v_out[part, :] = finish(wide, v_raw[part, :], v_inv[part, 0:1])
+
+        @pl.when(core == 0)
+        def _():
+            pltpu.make_async_copy(v_out.at[part], gi_ref.at[part], v_sem.at[slot]).start()
+
+        @pl.when(core == 1)
+        def _():
+            pltpu.make_async_copy(v_out.at[part], gt_ref.at[part], v_sem.at[slot]).start()
 
     pltpu.make_async_copy(u_out, gt_ref, u_sem).wait()
-    for slot in range(rows // STORE_ROWS):
+    for slot in range(slots):
         part = pl.ds(slot * STORE_ROWS, STORE_ROWS)
         pltpu.make_async_copy(v_out.at[part], gi_ref.at[part], v_sem.at[slot]).wait()
 
@@ -60,6 +67,10 @@
     v_grad,
     v_raw,
     v_inv,
+    last_unit,
+    last_weights,
+    scale_here,
+    bias_here,
     u_raw,
     chip_raw,
     near_raw,
@@ -86,13 +97,16 @@
     partner = me + 1 - 2 * core
     near_to = lax.rem(me + 4 * core - 2 + n, n)
     far_to = lax.rem(me + 2 * core - 1 + n, n)
-    scale = scale_ref[0]
-    bias = bias_ref[0]
 
     barrier = pltpu.get_barrier_semaphore()
     near_from = lax.rem(me + 2 - 4 * core + n, n)
     for sender in (partner, near_from, far_to):
         pl.semaphore_signal(barrier, inc=1, device_id=(sender,), device_id_type=MESH)
+
+    load_scale = pltpu.make_async_copy(scale_ref, scale_here, load_sem.at[2])
+    load_bias = pltpu.make_async_copy(bias_ref, bias_here, load_sem.at[3])
+    load_scale.start()
+    load_bias.start()
 
     def on_core(which, texts, images):
         @pl.when(core == which)
@@ -139,7 +153,7 @@
         )
 
     def send_far(k):
-        part = pl.ds(k * FAR_ROWS, FAR_ROWS)
+        part = pl.ds(*FAR_CHUNKS[k])
         return pltpu.make_async_remote_copy(
             src_ref=chip_raw.at[part],
             dst_ref=far_raw.at[part],
@@ -152,7 +166,8 @@
     on_core(0, txt_ref, img_ref)
     on_core(1, img_ref, txt_ref)
     send_chip(txt_ref).wait_recv()
-    for k in range(rows // FAR_ROWS):
+    fars = len(FAR_CHUNKS)
+    for k in range(fars):
         send_far(k).start()
 
     def normalize(raw, unit, start, count, inverses=None):
@@ -164,21 +179,24 @@
             if inverses is not None:
                 inverses[part, :] = jnp.broadcast_to(inverse, (part.size, inverses.shape[1]))
 
+    def weigh(own, part, diagonal=False):
+        logits = scale * lax.dot_general(
+            own, part, (((1,), (1,)), ((), ())), preferred_element_type=jnp.float32
+        ) + bias
+        if diagonal:
+            down = lax.broadcasted_iota(jnp.int32, logits.shape, 0)
+            across = lax.broadcasted_iota(jnp.int32, logits.shape, 1)
+            signs = jnp.where(down == across, jnp.float32(1.0), jnp.float32(-1.0))
+            slope = -signs * jax.nn.sigmoid(-signs * logits)
+        else:
+            slope = jax.nn.sigmoid(logits)
+        return (scale * slope).astype(jnp.bfloat16)
+
     def accumulate(own, block, start, count, grad, diagonal=False, first=False):
         part = block[pl.ds(start, count), :]
         for at in range(0, rows, TILE):
             here = pl.ds(at, TILE)
-            logits = scale * lax.dot_general(
-                own[here, :], part, (((1,), (1,)), ((), ())), preferred_element_type=jnp.float32
-            ) + bias
-            if diagonal and at == start:
-                down = lax.broadcasted_iota(jnp.int32, logits.shape, 0)
-                across = lax.broadcasted_iota(jnp.int32, logits.shape, 1)
-                signs = jnp.where(down == across, jnp.float32(1.0), jnp.float32(-1.0))
-                slope = -signs * jax.nn.sigmoid(-signs * logits)
-            else:
-                slope = jax.nn.sigmoid(logits)
-            weights = (scale * slope).astype(jnp.bfloat16)
+            weights = weigh(own[here, :], part, diagonal and at == start)
             term = jnp.dot(weights, part, preferred_element_type=jnp.float32)
             grad[here, :] = term if first else grad[here, :] + term
 
@@ -186,6 +204,10 @@
     pltpu.make_async_copy(img_ref, v_raw, load_sem.at[1]).wait()
     normalize(u_raw, u_unit, 0, rows, u_inv)
     normalize(v_raw, v_unit, 0, rows, v_inv)
+    load_scale.wait()
+    load_bias.wait()
+    scale = scale_here[0]
+    bias = bias_here[0]
     for start in range(0, rows, TILE):
         accumulate(u_unit, v_unit, start, TILE, u_grad, diagonal=True, first=start == 0)
         accumulate(v_unit, u_unit, start, TILE, v_grad, diagonal=True, first=start == 0)
@@ -196,7 +218,6 @@
 
     per_tile = TILE // NEAR_ROWS
     nears = rows // NEAR_ROWS
-    fars = rows // FAR_ROWS
     for tile in range(rows // TILE):
         for k in range(tile * per_tile, (tile + 1) * per_tile):
             send_near(img_ref, k).wait_recv()
@@ -208,12 +229,21 @@
             send_relay(k).wait_recv()
             normalize(relay_raw, block_unit, k * NEAR_ROWS, NEAR_ROWS)
         accumulate(v_unit, block_unit, tile * TILE, TILE, v_grad)
-    finish(u_grad, u_raw, u_inv, u_out, 0, rows)
+    for at in range(0, rows, 64):
+        here = pl.ds(at, 64)
+        u_out[here, :] = finish(u_grad[here, :], u_raw[here, :], u_inv[here, 0:1])
 
     for k in range(fars):
         send_far(k).wait_recv()
-        normalize(far_raw, block_unit, k * FAR_ROWS, FAR_ROWS)
-        accumulate(v_unit, block_unit, k * FAR_ROWS, FAR_ROWS, v_grad)
+        start, count = FAR_CHUNKS[k]
+        normalize(far_raw, block_unit, start, count)
+        if k + 1 < fars:
+            accumulate(v_unit, block_unit, start, count, v_grad)
+        else:
+            last_unit[...] = block_unit[pl.ds(start, count), :]
+            for at in range(0, rows, TILE):
+                here = pl.ds(at, TILE)
+                last_weights[here, :] = weigh(v_unit[here, :], last_unit[...])
 
     for k in range(nears):
         send_near(img_ref, k).wait_send()
@@ -232,22 +262,28 @@
         total = pltpu.VMEM((rows, depth), jnp.float32)
         inverses = pltpu.VMEM((rows, 128), jnp.float32)
         dma = pltpu.SemaphoreType.DMA
-        nears, fars = rows // NEAR_ROWS, rows // FAR_ROWS
+        nears, fars = rows // NEAR_ROWS, len(FAR_CHUNKS)
+        scalar = pltpu.SMEM((1,), jnp.float32)
+        last = pltpu.VMEM((LAST_ROWS, depth), jnp.bfloat16)
+        last_weights = pltpu.VMEM((rows, LAST_ROWS), jnp.bfloat16)
         in_vmem = pl.BlockSpec(memory_space=pltpu.VMEM)
         in_hbm = pl.BlockSpec(memory_space=pltpu.HBM)
-        images = pltpu.with_memory_space_constraint(images, pltpu.HBM)
-        texts = pltpu.with_memory_space_constraint(texts, pltpu.HBM)
+        operands = [
+            pltpu.with_memory_space_constraint(operand, pltpu.HBM)
+            for operand in (images, texts)
+        ]
         parts = pl.pallas_call(
             functools.partial(kernel, n),
-            out_shape=(block, total, block, inverses),
-            in_specs=[in_hbm] * 2 + [pl.BlockSpec(memory_space=pltpu.SMEM)] * 2,
-            out_specs=[in_vmem] * 4,
-            scratch_shapes=[block] * 5
+            out_shape=(block, total, block, inverses, last, last_weights),
+            in_specs=[in_hbm] * 2 + [pl.BlockSpec(memory_space=pl.ANY)] * 2,
+            out_specs=[in_vmem] * 6,
+            scratch_shapes=[scalar] * 2
+            + [block] * 5
             + [block] * 3
             + [inverses]
             + [total]
             + [
-                dma((2,)),
+                dma((4,)),
                 dma((1,)),
                 dma((1,)),
                 dma((nears,)),
@@ -263,13 +299,13 @@
             cost_estimate=pl.CostEstimate(
                 flops=24 * rows * rows * depth, bytes_accessed=8 * rows * depth, transcendentals=0
             ),
-        )(images, texts, logit_scale, logit_bias)
+        )(*operands, logit_scale, logit_bias)
         parts = [pltpu.with_memory_space_constraint(part, pltpu.VMEM) for part in parts]
         result = jax.ShapeDtypeStruct((rows, depth), jnp.bfloat16)
         return pl.pallas_call(
             finish_kernel,
             out_shape=(result, result),
-            in_specs=[in_vmem] * 4,
+            in_specs=[in_vmem] * 6,
             out_specs=[in_hbm] * 2,
             scratch_shapes=[block, dma, dma((rows // STORE_ROWS,))],
             compiler_params=pltpu.CompilerParams(vmem_limit_bytes=16 * 1024 * 1024),

time: 45.4 us -> 41.3 us (0.910)
  Pallas kernels: 43.2 us -> 38.8 us
    pallas_call x1, Pallas kernels: 41.2 us -> 37.2 us  [shards(): pl.pallas_call(functools.partial(kernel, n), out_shape=(block, total, blo...]
where the time goes in v3:
time: 41.3 us; the launch traced here: 40.8 us
  Pallas kernels  38.8 us (94%)
  between operations  1.93 us (5%)
    pallas_call x1, Pallas kernels, shards(): pl.pallas_call(functools.partial(kernel, n), out_shape=(block, total, blo...  37.2 us
    pallas_call x1, Pallas kernels, shards(): pl.pallas_call(finish_kernel, out_shape=(result, result), in_specs=[in_vm...  1.66 us

profile of v3, /device:TPU:1, one launch (start us, length us, event | category | flops | bytes accessed | tf_op | source)
XLA Modules:
  0.0 40.8 jit_solution(4825606281873366568)
XLA Ops:
  1.9 37.2 %shard_map.59 = (bf16[512,1024]{1,0:T(8,128)(2,1)S(1)}, f32[512,1024]{1,0:T(8,128)S(1)}, bf16[512,1024]{1,0:T(8,128)(2,1)S(1)}, f32[512,128]{1,0:T(8,128)S(1)}, ...) custom-call(bf16[512,1024]{1,0:T(8,128)(2,1)} %img_ref.1, bf16[512,1024]{1,0:T(8,128)(2,1)} %txt_ref.1, ...), custom_call_target="tpu_custom_call" | custom-call | flops 6442450944 | bytes 4194304 | tf_op jit(solution)/shard_map/pallas_call | solution.py:275
  39.1 1.7 %shard_map.60 = (bf16[512,1024]{1,0:T(8,128)(2,1)}, bf16[512,1024]{1,0:T(8,128)(2,1)}) custom-call(bf16[512,1024]{1,0:T(8,128)(2,1)S(1)} %get-tuple-element.8.u_out, f32[512,1024]{1,0:T(8,128)S(1)} %get-tuple-element.9.v_grad, bf16[512,1024]{1,0:T(8,128)(2,1)S(1)} %get-tuple-element.10.v_raw, f32[512,128]{1,0:T(8,128)S(1)} %get-tuple-element.11.v_inv, ...), custom_call_target="tpu_custom_call" | custom-call | flops 4194304 | bytes 2097152 | tf_op jit(solution)/shard_map/pallas_call | solution.py:305

commit v4 on v3

--- a/solution.py
+++ b/solution.py
@@ -11,8 +11,16 @@
 MESH = pl.DeviceIdType.MESH
 TILE = 256
 NEAR_ROWS = 128
-FAR_CHUNKS = ((0, 128), (128, 128), (256, 128), (384, 64), (448, 64))
+FAR_CHUNKS = ((0, 128), (128, 128), (256, 64), (320, 64), (384, 64), (448, 64))
+FAR_GROUPS = ((0,), (1,), (2, 3, 4), (5,))
 LAST_ROWS = FAR_CHUNKS[-1][1]
+LINE = 8
+HOP = 3
+DETOUR = (2, 3)
+DETOUR_ROWS = 64
+ENDS = 2 * LINE - 1
+BACK = (ENDS - 1, ENDS - 2 * HOP, ENDS - 4 * HOP, 0)
+FORTH = tuple(ENDS - spot for spot in BACK)
 STORE_ROWS = 128
 
 
@@ -90,6 +98,10 @@
     relay_recv,
     far_send,
     far_recv,
+    detour_raw,
+    detour_send,
+    detour_recv,
+    ready,
 ):
     rows, depth = u_raw.shape
     me = lax.axis_index("dp")
@@ -97,28 +109,94 @@
     partner = me + 1 - 2 * core
     near_to = lax.rem(me + 4 * core - 2 + n, n)
     far_to = lax.rem(me + 2 * core - 1 + n, n)
+    spot = lax.rem(me, 2 * LINE)
+    sign = 2 * core - 1
+
+    def away(by):
+        return lax.rem(me + by + n, n)
+
+    leaves = jnp.logical_or(spot >= ENDS - 1, spot == BACK[1])
+    from_last = jnp.logical_and(me >= n - 2 * LINE, leaves)
+    to_first = jnp.logical_and(me < 2 * LINE, jnp.logical_not(leaves))
+    back = jnp.where(jnp.logical_or(from_last, to_first), -1, spot)
+
+    def any_of(*conditions):
+        return functools.reduce(jnp.logical_or, conditions)
+
+    def back_at(*steps):
+        return any_of(*[back == BACK[step] for step in steps])
+
+    def forth_at(*steps):
+        return any_of(*[spot == FORTH[step] for step in steps])
+
+    lead_to = away(sign * (2 * HOP - 1))
+    hop_to = away(sign * (4 * HOP - 2))
+    home_to = away(-sign * HOP)
+    steps = (2 * HOP - 1, 2 - 4 * HOP, HOP)
+    skips = jnp.logical_or(back == FORTH[3], spot == BACK[3])
+    detours = jnp.logical_or(back_at(0, 1, 2), forth_at(0, 1, 2))
 
     barrier = pltpu.get_barrier_semaphore()
     near_from = lax.rem(me + 2 - 4 * core + n, n)
     for sender in (partner, near_from, far_to):
         pl.semaphore_signal(barrier, inc=1, device_id=(sender,), device_id_type=MESH)
+    for step, by in enumerate(steps):
+
+        @pl.when(back_at(step + 1))
+        def _():
+            pl.semaphore_signal(barrier, inc=1, device_id=(away(by),), device_id_type=MESH)
+
+        @pl.when(forth_at(step) if step < 2 else forth_at(3))
+        def _():
+            pl.semaphore_signal(
+                barrier,
+                inc=1,
+                device_id=(away(by if step < 2 else -by),),
+                device_id_type=MESH,
+            )
+
+    extra = [back_at(0), back_at(1), back_at(2), forth_at(1), forth_at(2), forth_at(2)]
+    signals = 3 + sum(one.astype(jnp.int32) for one in extra)
 
     load_scale = pltpu.make_async_copy(scale_ref, scale_here, load_sem.at[2])
     load_bias = pltpu.make_async_copy(bias_ref, bias_here, load_sem.at[3])
     load_scale.start()
     load_bias.start()
 
-    def on_core(which, texts, images):
+    def on_core(which, u_source, v_source):
         @pl.when(core == which)
         def _():
-            load_u = pltpu.make_async_copy(texts, u_raw, load_sem.at[0])
-            load_v = pltpu.make_async_copy(images, v_raw, load_sem.at[1])
+            load_u = pltpu.make_async_copy(u_source, u_raw, load_sem.at[0])
+            load_v = pltpu.make_async_copy(v_source, v_raw, load_sem.at[1])
             load_u.start()
             load_v.start()
-            pl.semaphore_wait(barrier, 3)
-            send_chip(texts).start()
-            for k in range(rows // NEAR_ROWS):
-                send_near(images, k).start()
+            pl.semaphore_wait(barrier, signals)
+            for by, receiver in zip(steps, FORTH[1:3]):
+                if receiver % 2 == which:
+
+                    @pl.when(spot == receiver)
+                    def _():
+                        pl.semaphore_signal(
+                            ready, inc=1, device_id=(away(-by),), device_id_type=MESH
+                        )
+
+            def lead():
+                for j, k in enumerate(DETOUR):
+                    send_detour(u_source.at[pl.ds(*FAR_CHUNKS[k])], j, lead_to).start()
+
+            if which == BACK[0] % 2:
+                pl.when(back_at(0))(lead)
+            send_chip(u_source).start()
+            nears = rows // NEAR_ROWS
+            for k in range(nears):
+                if which == FORTH[0] % 2 and k == nears // 2:
+
+                    @pl.when(spot == FORTH[0])
+                    def _():
+                        pl.semaphore_wait(ready, 1)
+                        lead()
+
+                send_near(v_source, k).start()
 
     def send_chip(source):
         return pltpu.make_async_remote_copy(
@@ -163,12 +241,43 @@
             device_id_type=MESH,
         )
 
+    def send_detour(source, j, to):
+        return pltpu.make_async_remote_copy(
+            src_ref=source,
+            dst_ref=detour_raw.at[pl.ds(j * DETOUR_ROWS, DETOUR_ROWS)],
+            send_sem=detour_send.at[j],
+            recv_sem=detour_recv.at[j],
+            device_id=(to,),
+            device_id_type=MESH,
+        )
+
+    def pass_detour(j, hop):
+        held = detour_raw.at[pl.ds(j * DETOUR_ROWS, DETOUR_ROWS)]
+
+        @pl.when(jnp.logical_or(back_at(hop), forth_at(hop)))
+        def _():
+            if j == 0 and hop == 1:
+
+                @pl.when(spot == FORTH[hop])
+                def _():
+                    pl.semaphore_wait(ready, 1)
+
+            send_detour(held, j, hop_to).wait_recv()
+            if hop == 1:
+                send_detour(held, j, hop_to).start()
+            else:
+                k = DETOUR[j]
+                pltpu.make_async_remote_copy(
+                    src_ref=held,
+                    dst_ref=far_raw.at[pl.ds(*FAR_CHUNKS[k])],
+                    send_sem=detour_send.at[j],
+                    recv_sem=far_recv.at[k],
+                    device_id=(home_to,),
+                    device_id_type=MESH,
+                ).start()
+
     on_core(0, txt_ref, img_ref)
     on_core(1, img_ref, txt_ref)
-    send_chip(txt_ref).wait_recv()
-    fars = len(FAR_CHUNKS)
-    for k in range(fars):
-        send_far(k).start()
 
     def normalize(raw, unit, start, count, inverses=None):
         for at in range(start, start + count, 64):
@@ -212,32 +321,52 @@
         accumulate(u_unit, v_unit, start, TILE, u_grad, diagonal=True, first=start == 0)
         accumulate(v_unit, u_unit, start, TILE, v_grad, diagonal=True, first=start == 0)
 
+    send_chip(txt_ref).wait_recv()
+    fars = len(FAR_CHUNKS)
+    for k in range(fars):
+        if k in DETOUR:
+            pl.when(jnp.logical_not(skips))(send_far(k).start)
+        else:
+            send_far(k).start()
+
     normalize(chip_raw, block_unit, 0, rows)
     for start in range(0, rows, TILE):
         accumulate(u_unit, block_unit, start, TILE, u_grad)
 
     per_tile = TILE // NEAR_ROWS
     nears = rows // NEAR_ROWS
+
+    def take_relay():
+        for tile in range(rows // TILE):
+            for k in range(tile * per_tile, (tile + 1) * per_tile):
+                send_relay(k).wait_recv()
+                normalize(relay_raw, block_unit, k * NEAR_ROWS, NEAR_ROWS)
+            accumulate(v_unit, block_unit, tile * TILE, TILE, v_grad)
+
+    near_late = spot == FORTH[0]
+    pl.when(near_late)(take_relay)
     for tile in range(rows // TILE):
         for k in range(tile * per_tile, (tile + 1) * per_tile):
             send_near(img_ref, k).wait_recv()
             send_relay(k).start()
+            if k % 2 == 0:
+                pass_detour(k // 2, 1)
             normalize(near_raw, block_unit, k * NEAR_ROWS, NEAR_ROWS)
         accumulate(u_unit, block_unit, tile * TILE, TILE, u_grad)
-    for tile in range(rows // TILE):
-        for k in range(tile * per_tile, (tile + 1) * per_tile):
-            send_relay(k).wait_recv()
-            normalize(relay_raw, block_unit, k * NEAR_ROWS, NEAR_ROWS)
-        accumulate(v_unit, block_unit, tile * TILE, TILE, v_grad)
+    pl.when(jnp.logical_not(near_late))(take_relay)
     for at in range(0, rows, 64):
         here = pl.ds(at, 64)
         u_out[here, :] = finish(u_grad[here, :], u_raw[here, :], u_inv[here, 0:1])
 
-    for k in range(fars):
-        send_far(k).wait_recv()
-        start, count = FAR_CHUNKS[k]
+    for g, chunks in enumerate(FAR_GROUPS):
+        for j in ((0, 1), (), (), ())[g]:
+            pass_detour(j, 2)
+        for k in chunks:
+            send_far(k).wait_recv()
+        start = FAR_CHUNKS[chunks[0]][0]
+        count = sum(FAR_CHUNKS[k][1] for k in chunks)
         normalize(far_raw, block_unit, start, count)
-        if k + 1 < fars:
+        if g + 1 < len(FAR_GROUPS):
             accumulate(v_unit, block_unit, start, count, v_grad)
         else:
             last_unit[...] = block_unit[pl.ds(start, count), :]
@@ -249,7 +378,16 @@
         send_near(img_ref, k).wait_send()
         send_relay(k).wait_send()
     for k in range(fars):
-        send_far(k).wait_send()
+        if k in DETOUR:
+            pl.when(jnp.logical_not(skips))(send_far(k).wait_send)
+        else:
+            send_far(k).wait_send()
+
+    @pl.when(detours)
+    def _():
+        for j in range(len(DETOUR)):
+            send_detour(detour_raw.at[pl.ds(j * DETOUR_ROWS, DETOUR_ROWS)], j, hop_to).wait_send()
+
     send_chip(txt_ref).wait_send()
 
 
@@ -292,6 +430,10 @@
                 dma((nears,)),
                 dma((fars,)),
                 dma((fars,)),
+                pltpu.VMEM((len(DETOUR) * DETOUR_ROWS, depth), jnp.bfloat16),
+                dma((len(DETOUR),)),
+                dma((len(DETOUR),)),
+                pltpu.SemaphoreType.REGULAR,
             ],
             compiler_params=pltpu.CompilerParams(
                 collective_id=0, has_side_effects=True, vmem_limit_bytes=40 * 1024 * 1024

time: 41.3 us -> 39 us (0.944)
  Pallas kernels: 38.8 us -> 36.8 us
    pallas_call x1, Pallas kernels: 37.2 us -> 35.1 us  [shards(): pl.pallas_call(functools.partial(kernel, n), out_shape=(block, total, blo...]
where the time goes in v4:
time: 39 us; the launch traced here: 38.9 us
  Pallas kernels  36.8 us (94%)
  between operations  2.09 us (5%)
    pallas_call x1, Pallas kernels, shards(): pl.pallas_call(functools.partial(kernel, n), out_shape=(block, total, blo...  35.1 us
    pallas_call x1, Pallas kernels, shards(): pl.pallas_call(finish_kernel, out_shape=(result, result), in_specs=[in_vm...  1.67 us

profile of v4, /device:TPU:1, one launch (start us, length us, event | category | flops | bytes accessed | tf_op | source)
XLA Modules:
  0.0 38.9 jit_solution(8762808865241283129)
XLA Ops:
  1.9 35.1 %shard_map.59 = (bf16[512,1024]{1,0:T(8,128)(2,1)S(1)}, f32[512,1024]{1,0:T(8,128)S(1)}, bf16[512,1024]{1,0:T(8,128)(2,1)S(1)}, f32[512,128]{1,0:T(8,128)S(1)}, ...) custom-call(bf16[512,1024]{1,0:T(8,128)(2,1)} %img_ref.1, bf16[512,1024]{1,0:T(8,128)(2,1)} %txt_ref.1, ...), custom_call_target="tpu_custom_call" | custom-call | flops 6442450944 | bytes 4194304 | tf_op jit(solution)/shard_map/pallas_call | solution.py:413
  37.0 1.7 %shard_map.60 = (bf16[512,1024]{1,0:T(8,128)(2,1)}, bf16[512,1024]{1,0:T(8,128)(2,1)}) custom-call(bf16[512,1024]{1,0:T(8,128)(2,1)S(1)} %get-tuple-element.8.u_out, f32[512,1024]{1,0:T(8,128)S(1)} %get-tuple-element.9.v_grad, bf16[512,1024]{1,0:T(8,128)(2,1)S(1)} %get-tuple-element.10.v_raw, f32[512,128]{1,0:T(8,128)S(1)} %get-tuple-element.11.v_inv, ...), custom_call_target="tpu_custom_call" | custom-call | flops 4194304 | bytes 2097152 | tf_op jit(solution)/shard_map/pallas_call | solution.py:447

commit v5 on v4

--- a/solution.py
+++ b/solution.py
@@ -11,13 +11,13 @@
 MESH = pl.DeviceIdType.MESH
 TILE = 256
 NEAR_ROWS = 128
-FAR_CHUNKS = ((0, 128), (128, 128), (256, 64), (320, 64), (384, 64), (448, 64))
+FAR_CHUNKS = ((0, 128), (128, 96), (224, 80), (304, 80), (384, 64), (448, 64))
 FAR_GROUPS = ((0,), (1,), (2, 3, 4), (5,))
 LAST_ROWS = FAR_CHUNKS[-1][1]
 LINE = 8
 HOP = 3
 DETOUR = (2, 3)
-DETOUR_ROWS = 64
+DETOUR_ROWS = 80
 ENDS = 2 * LINE - 1
 BACK = (ENDS - 1, ENDS - 2 * HOP, ENDS - 4 * HOP, 0)
 FORTH = tuple(ENDS - spot for spot in BACK)
@@ -102,6 +102,7 @@
     detour_send,
     detour_recv,
     ready,
+    mate,
 ):
     rows, depth = u_raw.shape
     me = lax.axis_index("dp")
@@ -138,7 +139,11 @@
 
     barrier = pltpu.get_barrier_semaphore()
     near_from = lax.rem(me + 2 - 4 * core + n, n)
-    for sender in (partner, near_from, far_to):
+    @pl.when(core == 1)
+    def _():
+        pl.semaphore_signal(barrier, inc=1, device_id=(partner,), device_id_type=MESH)
+
+    for sender in (near_from, far_to):
         pl.semaphore_signal(barrier, inc=1, device_id=(sender,), device_id_type=MESH)
     for step, by in enumerate(steps):
 
@@ -156,7 +161,7 @@
             )
 
     extra = [back_at(0), back_at(1), back_at(2), forth_at(1), forth_at(2), forth_at(2)]
-    signals = 3 + sum(one.astype(jnp.int32) for one in extra)
+    signals = 3 - core + sum(one.astype(jnp.int32) for one in extra)
 
     load_scale = pltpu.make_async_copy(scale_ref, scale_here, load_sem.at[2])
     load_bias = pltpu.make_async_copy(bias_ref, bias_here, load_sem.at[3])
@@ -186,7 +191,9 @@
 
             if which == BACK[0] % 2:
                 pl.when(back_at(0))(lead)
-            send_chip(u_source).start()
+            if which == 0:
+                pl.semaphore_signal(mate, inc=1, device_id=(partner,), device_id_type=MESH)
+                send_chip(u_source).start()
             nears = rows // NEAR_ROWS
             for k in range(nears):
                 if which == FORTH[0] % 2 and k == nears // 2:
@@ -280,8 +287,9 @@
     on_core(1, img_ref, txt_ref)
 
     def normalize(raw, unit, start, count, inverses=None):
-        for at in range(start, start + count, 64):
-            part = pl.ds(at, min(64, count))
+        step = 64 if count % 64 == 0 else 32
+        for at in range(start, start + count, step):
+            part = pl.ds(at, step)
             wide = raw[part, :].astype(jnp.float32)
             inverse = lax.rsqrt(jnp.sum(wide * wide, axis=1, keepdims=True) + EPS)
             unit[part, :] = (wide * inverse).astype(jnp.bfloat16)
@@ -320,6 +328,11 @@
     for start in range(0, rows, TILE):
         accumulate(u_unit, v_unit, start, TILE, u_grad, diagonal=True, first=start == 0)
         accumulate(v_unit, u_unit, start, TILE, v_grad, diagonal=True, first=start == 0)
+
+    @pl.when(core == 1)
+    def _():
+        pl.semaphore_wait(mate, 1)
+        send_chip(img_ref).start()
 
     send_chip(txt_ref).wait_recv()
     fars = len(FAR_CHUNKS)
@@ -434,6 +447,7 @@
                 dma((len(DETOUR),)),
                 dma((len(DETOUR),)),
                 pltpu.SemaphoreType.REGULAR,
+                pltpu.SemaphoreType.REGULAR,
             ],
             compiler_params=pltpu.CompilerParams(
                 collective_id=0, has_side_effects=True, vmem_limit_bytes=40 * 1024 * 1024

time: 39 us -> 38.5 us (0.987)
  Pallas kernels: 36.8 us -> 36.2 us
    pallas_call x1, Pallas kernels: 35.1 us -> 34.6 us  [shards(): pl.pallas_call(functools.partial(kernel, n), out_shape=(block, total, blo...]
where the time goes in v5:
time: 38.5 us; the launch traced here: 38.3 us
  Pallas kernels  36.2 us (94%)
  between operations  2.09 us (5%)
    pallas_call x1, Pallas kernels, shards(): pl.pallas_call(functools.partial(kernel, n), out_shape=(block, total, blo...  34.6 us
    pallas_call x1, Pallas kernels, shards(): pl.pallas_call(finish_kernel, out_shape=(result, result), in_specs=[in_vm...  1.66 us

profile of v5, /device:TPU:1, one launch (start us, length us, event | category | flops | bytes accessed | tf_op | source)
XLA Modules:
  0.0 38.3 jit_solution(7761263633935181923)
XLA Ops:
  1.9 34.6 %shard_map.59 = (bf16[512,1024]{1,0:T(8,128)(2,1)S(1)}, f32[512,1024]{1,0:T(8,128)S(1)}, bf16[512,1024]{1,0:T(8,128)(2,1)S(1)}, f32[512,128]{1,0:T(8,128)S(1)}, ...) custom-call(bf16[512,1024]{1,0:T(8,128)(2,1)} %img_ref.1, bf16[512,1024]{1,0:T(8,128)(2,1)} %txt_ref.1, ...), custom_call_target="tpu_custom_call" | custom-call | flops 6442450944 | bytes 4194304 | tf_op jit(solution)/shard_map/pallas_call | solution.py:426
  36.5 1.7 %shard_map.60 = (bf16[512,1024]{1,0:T(8,128)(2,1)}, bf16[512,1024]{1,0:T(8,128)(2,1)}) custom-call(bf16[512,1024]{1,0:T(8,128)(2,1)S(1)} %get-tuple-element.8.u_out, f32[512,1024]{1,0:T(8,128)S(1)} %get-tuple-element.9.v_grad, bf16[512,1024]{1,0:T(8,128)(2,1)S(1)} %get-tuple-element.10.v_raw, f32[512,128]{1,0:T(8,128)S(1)} %get-tuple-element.11.v_inv, ...), custom_call_target="tpu_custom_call" | custom-call | flops 4194304 | bytes 2097152 | tf_op jit(solution)/shard_map/pallas_call | solution.py:461

commit v6 on v5

--- a/solution.py
+++ b/solution.py
@@ -12,7 +12,7 @@
 TILE = 256
 NEAR_ROWS = 128
 FAR_CHUNKS = ((0, 128), (128, 96), (224, 80), (304, 80), (384, 64), (448, 64))
-FAR_GROUPS = ((0,), (1,), (2, 3, 4), (5,))
+FAR_GROUPS = ((0, 1), (2, 3, 4), (5,))
 LAST_ROWS = FAR_CHUNKS[-1][1]
 LINE = 8
 HOP = 3
@@ -372,7 +372,7 @@
         u_out[here, :] = finish(u_grad[here, :], u_raw[here, :], u_inv[here, 0:1])
 
     for g, chunks in enumerate(FAR_GROUPS):
-        for j in ((0, 1), (), (), ())[g]:
+        for j in ((0, 1), (), ())[g]:
             pass_detour(j, 2)
         for k in chunks:
             send_far(k).wait_recv()

time: 38.5 us -> 38.3 us (level)
  no operation moved by 1% of the time
where the time goes in v6:
time: 38.3 us; the launch traced here: 38.1 us
  Pallas kernels  36.1 us (94%)
  between operations  2.09 us (5%)
    pallas_call x1, Pallas kernels, shards(): pl.pallas_call(functools.partial(kernel, n), out_shape=(block, total, blo...  34.4 us
    pallas_call x1, Pallas kernels, shards(): pl.pallas_call(finish_kernel, out_shape=(result, result), in_specs=[in_vm...  1.67 us

profile of v6, /device:TPU:1, one launch (start us, length us, event | category | flops | bytes accessed | tf_op | source)
XLA Modules:
  0.0 38.1 jit_solution(5288826745838345167)
XLA Ops:
  1.9 34.4 %shard_map.59 = (bf16[512,1024]{1,0:T(8,128)(2,1)S(1)}, f32[512,1024]{1,0:T(8,128)S(1)}, bf16[512,1024]{1,0:T(8,128)(2,1)S(1)}, f32[512,128]{1,0:T(8,128)S(1)}, ...) custom-call(bf16[512,1024]{1,0:T(8,128)(2,1)} %img_ref.1, bf16[512,1024]{1,0:T(8,128)(2,1)} %txt_ref.1, ...), custom_call_target="tpu_custom_call" | custom-call | flops 6442450944 | bytes 4194304 | tf_op jit(solution)/shard_map/pallas_call | solution.py:426
  36.3 1.7 %shard_map.60 = (bf16[512,1024]{1,0:T(8,128)(2,1)}, bf16[512,1024]{1,0:T(8,128)(2,1)}) custom-call(bf16[512,1024]{1,0:T(8,128)(2,1)S(1)} %get-tuple-element.8.u_out, f32[512,1024]{1,0:T(8,128)S(1)} %get-tuple-element.9.v_grad, bf16[512,1024]{1,0:T(8,128)(2,1)S(1)} %get-tuple-element.10.v_raw, f32[512,128]{1,0:T(8,128)S(1)} %get-tuple-element.11.v_inv, ...), custom_call_target="tpu_custom_call" | custom-call | flops 4194304 | bytes 2097152 | tf_op jit(solution)/shard_map/pallas_call | solution.py:461
